TPU v7x, 256 devices: a whole 4x4x8 slice. The times are simulated.
256 devices in a mesh: query: 8 (over z), doc: 16 (over x, y), tok: 2 (over core).
Axes of the slice: x: 4, y: 4, z: 8, core: 2. Of those that a mesh axis runs over, the one named last changes fastest.
Arguments:
- queries: bfloat16 [2048, 32, 128], P(('query', 'doc'), 'tok'), may hold values from -14 to 14
- documents: bfloat16 [512, 128, 128], P(('query', 'doc')), may hold values from -14 to 14
- doc_lengths: int32 [512], P(('query', 'doc')), may hold values from 1 to 128, 40960 in all
- candidates: int32 [256, 256], P(('query', 'doc')), may hold values from 0 to 511, all different within a row
Outputs:
- top_scores: float32 [2048, 128], P(('query', 'doc'))
Inputs may be any that keep to these rules, and one draw needn't show every extreme that they name: `candidates`: each row names 256 different document block ids; every id appears in some row. `doc_lengths`: the counts sum to 40960.
All inputs are finite; a program needn't handle non-finite values. No bound on the sum of `doc_lengths` on one device may be relied on, other than what follows from the above.
Results may differ from a plain program's by a relative error of at most 0.0003.
Values may be sent and summed in bfloat16 or wider, within the bound.
A program may use at most 64 MiB of HBM per device.

v0:
```python
import jax
import jax.numpy as jnp
from jax import lax
from jax.sharding import PartitionSpec as P

QBLK = 8


epsilon = 1e-06
absent_score = -10000.0
excluded_score = -1e30


def joined(value, axis, join):
    pieces = lax.all_gather(value, axis)
    head = pieces[0]
    tail = pieces[1:]
    total, _ = lax.scan(lambda total, slab: (join(total, slab), None), head, tail)
    return total


def unit_rows(values):
    widened = values.astype(jnp.float32)
    scale = lax.rsqrt(jnp.sum(widened * widened, axis=-1, keepdims=True) + epsilon)
    return (widened * scale).astype(jnp.bfloat16)


def block_size():
    return 4


def maxsim(query_rows, docs, lengths):
    doc_count = docs.shape[0]
    block_width = block_size()
    row_count = query_rows.shape[0]
    query_tokens = query_rows.shape[1]
    flat_queries = query_rows.reshape(row_count * query_tokens, query_rows.shape[2])
    doc_tokens = docs.shape[1]
    blocked_docs = docs.reshape(doc_count // block_width, block_width * doc_tokens, docs.shape[2])
    blocked_lengths = lengths.reshape(doc_count // block_width, block_width)
    positions = jnp.arange(doc_tokens, dtype=jnp.int32)

    def one_block(operands):
        block_docs, block_lengths = operands
        similar = lax.dot_general(
            flat_queries, block_docs, (((1,), (1,)), ((), ())), preferred_element_type=jnp.float32
        )
        similar = similar.reshape(row_count, query_tokens, block_width, doc_tokens)
        live_mask = positions[None, :] < block_lengths[:, None]
        similar = jnp.where(live_mask[None, None], similar, absent_score)
        return jnp.sum(jnp.max(similar, axis=3), axis=1).T

    return lax.map(one_block, (blocked_docs, blocked_lengths)).reshape(doc_count, row_count)


def rank_rows(row_scores, lists, doc_ids, keep_count):
    live_mask = jnp.any(lists[:, :, None] == doc_ids[None, None, :], axis=1)
    live_mask = jnp.repeat(live_mask, QBLK, axis=0)
    masked = jnp.where(live_mask, row_scores, excluded_score)
    padding = jnp.full((masked.shape[0], keep_count - masked.shape[1]), excluded_score, jnp.float32)
    masked = jnp.concatenate([masked, padding], axis=1)
    return lax.top_k(masked, keep_count)[0]


def keep_best(first_list, second_list):
    return lax.top_k(jnp.concatenate([first_list, second_list], axis=1), first_list.shape[1])[0]


def body(queries, documents, doc_lengths, candidates):
    query_unit = unit_rows(queries)
    doc_unit = unit_rows(documents)
    own_queries = queries.shape[0]
    own_docs = documents.shape[0]
    query_devices = lax.axis_size("query")
    doc_devices = lax.axis_size("doc")
    all_docs = own_docs * query_devices * doc_devices
    keep_count = all_docs // 4
    query_group = lax.all_gather(query_unit, "doc", axis=0, tiled=True)
    doc_here = lax.axis_index("doc")
    block_scores = maxsim(
        query_group,
        lax.all_gather(doc_unit, "query", axis=0, tiled=True),
        lax.all_gather(doc_lengths, "query", axis=0, tiled=True),
    )
    scores = lax.psum(block_scores, "tok")
    group_docs = jnp.arange(own_docs * query_devices, dtype=jnp.int32)
    source_shard = group_docs // own_docs
    within = group_docs % own_docs
    group_ids = (source_shard * doc_devices + doc_here) * own_docs + within
    group_lists = lax.all_gather(candidates, "doc", axis=0, tiled=True)
    local_best = rank_rows(scores.T, group_lists, group_ids, keep_count)
    merged = joined(local_best, "doc", keep_best)
    result = lax.dynamic_slice_in_dim(merged, doc_here * own_queries, own_queries, 0)
    return result


def solution(mesh):
    in_specs = (
        P(("query", "doc"), "tok", None),
        P(("query", "doc"), None, None),
        P(("query", "doc")),
        P(("query", "doc"), None),
    )
    out_specs = P(("query", "doc"), None)
    return jax.shard_map(body, mesh=mesh, in_specs=in_specs, out_specs=out_specs, check_vma=False)
```

profile of v0, /device:TPU:1, one launch (start us, length us, event | category | flops | bytes accessed | tf_op | source)
XLA Modules:
  0.0 537.4 jit_solution(8718560259019842358)
XLA Ops:
  14.8 14.1 %all-reduce.1 = s32[32]{0:T(128)S(1)} all-reduce(s32[32]{0:T(128)S(1)} %dynamic-update-slice), channel_id=1, replica_groups=mesh['query'=8,'doc'=16,'tok'=2] {'query'}, use_global_device_ids=true, to_apply=%add.1 | all-reduce | flops 32 | bytes 256
  29.0 19.4 %all-gather.1 = s32[16,2,256]{2,1,0:T(2,128)S(1)} all-gather(s32[1,2,256]{2,1,0:T(2,128)} %bitcast.38), channel_id=1, replica_groups=mesh['query'=8,'doc'=16,'tok'=2] {'doc'}, dimensions={0}, use_global_device_ids=true | all-gather | bytes 34816 | tf_op jit(solution)/shard_map/all_gather | solution.py:90
  49.3 50.0 %all-gather.8.cloned.1.call-done = bf16[256,16,128]{2,1,0:T(8,128)(2,1)} async-done(((bf16[16,16,128]{2,1,0:T(8,128)(2,1)}), bf16[256,16,128]{2,1,0:T(8,128)(2,1)}) %all-gather.8.cloned.1.call-update) | async-done | bytes 1048592 | tf_op jit(solution)/shard_map/all_gather | solution.py:78
  99.2 266.1 %while.22 = (s32[]{:T(128)}, f32[8,4,256]{2,1,0:T(4,128)S(1)}, s32[8,4]{1,0:T(8,128)S(1)}, bf16[8,512,128]{2,1,0:T(8,128)(2,1)}, bf16[4096,128]{1,0:T(8,128)(2,1)}, /*index=5*/s32[]{:T(128)}, f32[]{:T(128)}) while((s32[]{:T(128)}, f32[8,4,256]{2,1,0:T(4,128)S(1)}, s32[8,4]{1,0:T(8,128)S(1)}, bf16[8,512,128]{2,1,0:T(8,128)(2,1)}, ...), condition=%wide.region_6.7_spmd.clone, body=%wide.region_3.0_spmd.clone.sunk | while | flops 541064704 | bytes 51664020 | solution.py:53
  105.0 9.0 %copy.32 = f32[4096,512]{1,0:T(8,128)} copy(f32[4096,512]{0,1:T(8,128)} %convolution_bitcast_fusion.2) | data formatting | bytes 16777216 | tf_op jit(solution)/shard_map/while/body/eval_jaxpr/dot_general | solution.py:45
  114.0 9.9 %reshape.103 = f32[256,16,4,128]{3,2,1,0:T(4,128)} reshape(f32[4096,512]{1,0:T(8,128)} %copy.32) | data formatting | bytes 16777216 | tf_op jit(solution)/shard_map/while/body/eval_jaxpr/reshape | solution.py:48
  124.0 7.9 %select_reduce_fusion.2 = f32[256,16,4]{2,1,0:T(8,128)S(1)} fusion(f32[256,16,4,128]{3,2,1,0:T(4,128)} %reshape.103, pred[4,128]{1,0:T(4,128)(4,1)S(1)} %iota_compare_fusion.2), kind=kLoop, calls=%fused_computation.3.clone.1 | loop fusion | flops 4177920 | bytes 8454656 | tf_op jit(solution)/shard_map/while/body/eval_jaxpr/reduce_max | solution.py:51
  132.5 5.8 %convolution_bitcast_fusion.2 = f32[4096,512]{0,1:T(8,128)} fusion(bf16[4096,128]{1,0:T(8,128)(2,1)} %get-tuple-element.163, bf16[8,512,128]{2,1,0:T(8,128)(2,1)} %get-tuple-element.162, s32[]{:T(128)S(6)} %copy.38), kind=kOutput, calls=%fused_computation.4.clone.1 | convolution fusion | flops 536870912 | bytes 9568260 | tf_op jit(solution)/shard_map/while/body/eval_jaxpr/dot_general | solution.py:45
  138.3 9.0 %copy.32 = f32[4096,512]{1,0:T(8,128)} copy(f32[4096,512]{0,1:T(8,128)} %convolution_bitcast_fusion.2) | data formatting | bytes 16777216 | tf_op jit(solution)/shard_map/while/body/eval_jaxpr/dot_general | solution.py:45
  147.3 9.9 %reshape.103 = f32[256,16,4,128]{3,2,1,0:T(4,128)} reshape(f32[4096,512]{1,0:T(8,128)} %copy.32) | data formatting | bytes 16777216 | tf_op jit(solution)/shard_map/while/body/eval_jaxpr/reshape | solution.py:48
  157.3 7.9 %select_reduce_fusion.2 = f32[256,16,4]{2,1,0:T(8,128)S(1)} fusion(f32[256,16,4,128]{3,2,1,0:T(4,128)} %reshape.103, pred[4,128]{1,0:T(4,128)(4,1)S(1)} %iota_compare_fusion.2), kind=kLoop, calls=%fused_computation.3.clone.1 | loop fusion | flops 4177920 | bytes 8454656 | tf_op jit(solution)/shard_map/while/body/eval_jaxpr/reduce_max | solution.py:51
  165.8 5.8 %convolution_bitcast_fusion.2 = f32[4096,512]{0,1:T(8,128)} fusion(bf16[4096,128]{1,0:T(8,128)(2,1)} %get-tuple-element.163, bf16[8,512,128]{2,1,0:T(8,128)(2,1)} %get-tuple-element.162, s32[]{:T(128)S(6)} %copy.38), kind=kOutput, calls=%fused_computation.4.clone.1 | convolution fusion | flops 536870912 | bytes 9568260 | tf_op jit(solution)/shard_map/while/body/eval_jaxpr/dot_general | solution.py:45
  171.5 9.0 %copy.32 = f32[4096,512]{1,0:T(8,128)} copy(f32[4096,512]{0,1:T(8,128)} %convolution_bitcast_fusion.2) | data formatting | bytes 16777216 | tf_op jit(solution)/shard_map/while/body/eval_jaxpr/dot_general | solution.py:45
  180.5 9.9 %reshape.103 = f32[256,16,4,128]{3,2,1,0:T(4,128)} reshape(f32[4096,512]{1,0:T(8,128)} %copy.32) | data formatting | bytes 16777216 | tf_op jit(solution)/shard_map/while/body/eval_jaxpr/reshape | solution.py:48
  190.6 7.9 %select_reduce_fusion.2 = f32[256,16,4]{2,1,0:T(8,128)S(1)} fusion(f32[256,16,4,128]{3,2,1,0:T(4,128)} %reshape.103, pred[4,128]{1,0:T(4,128)(4,1)S(1)} %iota_compare_fusion.2), kind=kLoop, calls=%fused_computation.3.clone.1 | loop fusion | flops 4177920 | bytes 8454656 | tf_op jit(solution)/shard_map/while/body/eval_jaxpr/reduce_max | solution.py:51
  204.8 9.0 %copy.32 = f32[4096,512]{1,0:T(8,128)} copy(f32[4096,512]{0,1:T(8,128)} %convolution_bitcast_fusion.2) | data formatting | bytes 16777216 | tf_op jit(solution)/shard_map/while/body/eval_jaxpr/dot_general | solution.py:45
  213.8 9.9 %reshape.103 = f32[256,16,4,128]{3,2,1,0:T(4,128)} reshape(f32[4096,512]{1,0:T(8,128)} %copy.32) | data formatting | bytes 16777216 | tf_op jit(solution)/shard_map/while/body/eval_jaxpr/reshape | solution.py:48
  223.8 7.9 %select_reduce_fusion.2 = f32[256,16,4]{2,1,0:T(8,128)S(1)} fusion(f32[256,16,4,128]{3,2,1,0:T(4,128)} %reshape.103, pred[4,128]{1,0:T(4,128)(4,1)S(1)} %iota_compare_fusion.2), kind=kLoop, calls=%fused_computation.3.clone.1 | loop fusion | flops 4177920 | bytes 8454656 | tf_op jit(solution)/shard_map/while/body/eval_jaxpr/reduce_max | solution.py:51
  238.1 9.0 %copy.32 = f32[4096,512]{1,0:T(8,128)} copy(f32[4096,512]{0,1:T(8,128)} %convolution_bitcast_fusion.2) | data formatting | bytes 16777216 | tf_op jit(solution)/shard_map/while/body/eval_jaxpr/dot_general | solution.py:45
  247.1 9.9 %reshape.103 = f32[256,16,4,128]{3,2,1,0:T(4,128)} reshape(f32[4096,512]{1,0:T(8,128)} %copy.32) | data formatting | bytes 16777216 | tf_op jit(solution)/shard_map/while/body/eval_jaxpr/reshape | solution.py:48
  257.1 7.9 %select_reduce_fusion.2 = f32[256,16,4]{2,1,0:T(8,128)S(1)} fusion(f32[256,16,4,128]{3,2,1,0:T(4,128)} %reshape.103, pred[4,128]{1,0:T(4,128)(4,1)S(1)} %iota_compare_fusion.2), kind=kLoop, calls=%fused_computation.3.clone.1 | loop fusion | flops 4177920 | bytes 8454656 | tf_op jit(solution)/shard_map/while/body/eval_jaxpr/reduce_max | solution.py:51
  271.3 9.0 %copy.32 = f32[4096,512]{1,0:T(8,128)} copy(f32[4096,512]{0,1:T(8,128)} %convolution_bitcast_fusion.2) | data formatting | bytes 16777216 | tf_op jit(solution)/shard_map/while/body/eval_jaxpr/dot_general | solution.py:45
  280.3 9.9 %reshape.103 = f32[256,16,4,128]{3,2,1,0:T(4,128)} reshape(f32[4096,512]{1,0:T(8,128)} %copy.32) | data formatting | bytes 16777216 | tf_op jit(solution)/shard_map/while/body/eval_jaxpr/reshape | solution.py:48
  290.4 7.9 %select_reduce_fusion.2 = f32[256,16,4]{2,1,0:T(8,128)S(1)} fusion(f32[256,16,4,128]{3,2,1,0:T(4,128)} %reshape.103, pred[4,128]{1,0:T(4,128)(4,1)S(1)} %iota_compare_fusion.2), kind=kLoop, calls=%fused_computation.3.clone.1 | loop fusion | flops 4177920 | bytes 8454656 | tf_op jit(solution)/shard_map/while/body/eval_jaxpr/reduce_max | solution.py:51
  304.6 9.0 %copy.32 = f32[4096,512]{1,0:T(8,128)} copy(f32[4096,512]{0,1:T(8,128)} %convolution_bitcast_fusion.2) | data formatting | bytes 16777216 | tf_op jit(solution)/shard_map/while/body/eval_jaxpr/dot_general | solution.py:45
  313.6 9.9 %reshape.103 = f32[256,16,4,128]{3,2,1,0:T(4,128)} reshape(f32[4096,512]{1,0:T(8,128)} %copy.32) | data formatting | bytes 16777216 | tf_op jit(solution)/shard_map/while/body/eval_jaxpr/reshape | solution.py:48
  323.6 7.9 %select_reduce_fusion.2 = f32[256,16,4]{2,1,0:T(8,128)S(1)} fusion(f32[256,16,4,128]{3,2,1,0:T(4,128)} %reshape.103, pred[4,128]{1,0:T(4,128)(4,1)S(1)} %iota_compare_fusion.2), kind=kLoop, calls=%fused_computation.3.clone.1 | loop fusion | flops 4177920 | bytes 8454656 | tf_op jit(solution)/shard_map/while/body/eval_jaxpr/reduce_max | solution.py:51
  337.9 9.0 %copy.32 = f32[4096,512]{1,0:T(8,128)} copy(f32[4096,512]{0,1:T(8,128)} %convolution_bitcast_fusion.2) | data formatting | bytes 16777216 | tf_op jit(solution)/shard_map/while/body/eval_jaxpr/dot_general | solution.py:45
  346.9 9.9 %reshape.103 = f32[256,16,4,128]{3,2,1,0:T(4,128)} reshape(f32[4096,512]{1,0:T(8,128)} %copy.32) | data formatting | bytes 16777216 | tf_op jit(solution)/shard_map/while/body/eval_jaxpr/reshape | solution.py:48
  356.9 7.9 %select_reduce_fusion.2 = f32[256,16,4]{2,1,0:T(8,128)S(1)} fusion(f32[256,16,4,128]{3,2,1,0:T(4,128)} %reshape.103, pred[4,128]{1,0:T(4,128)(4,1)S(1)} %iota_compare_fusion.2), kind=kLoop, calls=%fused_computation.3.clone.1 | loop fusion | flops 4177920 | bytes 8454656 | tf_op jit(solution)/shard_map/while/body/eval_jaxpr/reduce_max | solution.py:51
  365.5 5.9 %psum.7 = f32[256,32]{1,0:T(8,128)S(1)} all-reduce(f32[256,32]{1,0:T(8,128)S(1)} %bitcast.36), channel_id=1, replica_groups=mesh['query'=8,'doc'=16,'tok'=2] {'tok'}, use_global_device_ids=true, to_apply=%region_7.8 | all-reduce | flops 8192 | bytes 65536 | tf_op jit(solution)/shard_map/psum | solution.py:85
  375.3 48.1 %all-gather.10.cloned.1.call-done = f32[4096,128]{1,0:T(8,128)} async-done(((f32[256,128]{1,0:T(8,128)}), f32[4096,128]{1,0:T(8,128)}) %all-gather.10.cloned.1.call-update) | async-done | bytes 2097168 | tf_op jit(solution)/shard_map/all_gather | solution.py:15
  426.0 104.3 %while.21 = (s32[]{:T(128)}, f32[256,128]{1,0:T(8,128)S(1)}, f32[15,256,128]{2,1,0:T(8,128)S(1)}, s32[]{:T(128)}) while((s32[]{:T(128)}, f32[256,128]{1,0:T(8,128)S(1)}, f32[15,256,128]{2,1,0:T(8,128)S(1)}, s32[]{:T(128)}) %tuple.49), condition=%wide.region_11.12_spmd, body=%wide.region_9.11_spmd.sunk | while | flops 1114114 | bytes 3407937 | solution.py:18
  426.2 6.6 %top_k.21 = (f32[256,256]{0,1:T(8,128)S(1)}, s32[256,256]{0,1:T(8,128)}) sort(f32[256,256]{0,1:T(8,128)S(1)} %copy.30, s32[256,256]{0,1:T(8,128)S(1)} %iota.11.clone.2), dimensions={1}, to_apply=%region_10.10 | sort | flops 1048576 | bytes 1048576 | tf_op jit(solution)/shard_map/while/body/eval_jaxpr/top_k | solution.py:66
  433.2 6.6 %top_k.21 = (f32[256,256]{0,1:T(8,128)S(1)}, s32[256,256]{0,1:T(8,128)}) sort(f32[256,256]{0,1:T(8,128)S(1)} %copy.30, s32[256,256]{0,1:T(8,128)S(1)} %iota.11.clone.2), dimensions={1}, to_apply=%region_10.10 | sort | flops 1048576 | bytes 1048576 | tf_op jit(solution)/shard_map/while/body/eval_jaxpr/top_k | solution.py:66
  440.1 6.6 %top_k.21 = (f32[256,256]{0,1:T(8,128)S(1)}, s32[256,256]{0,1:T(8,128)}) sort(f32[256,256]{0,1:T(8,128)S(1)} %copy.30, s32[256,256]{0,1:T(8,128)S(1)} %iota.11.clone.2), dimensions={1}, to_apply=%region_10.10 | sort | flops 1048576 | bytes 1048576 | tf_op jit(solution)/shard_map/while/body/eval_jaxpr/top_k | solution.py:66
  447.1 6.6 %top_k.21 = (f32[256,256]{0,1:T(8,128)S(1)}, s32[256,256]{0,1:T(8,128)}) sort(f32[256,256]{0,1:T(8,128)S(1)} %copy.30, s32[256,256]{0,1:T(8,128)S(1)} %iota.11.clone.2), dimensions={1}, to_apply=%region_10.10 | sort | flops 1048576 | bytes 1048576 | tf_op jit(solution)/shard_map/while/body/eval_jaxpr/top_k | solution.py:66
  454.0 6.6 %top_k.21 = (f32[256,256]{0,1:T(8,128)S(1)}, s32[256,256]{0,1:T(8,128)}) sort(f32[256,256]{0,1:T(8,128)S(1)} %copy.30, s32[256,256]{0,1:T(8,128)S(1)} %iota.11.clone.2), dimensions={1}, to_apply=%region_10.10 | sort | flops 1048576 | bytes 1048576 | tf_op jit(solution)/shard_map/while/body/eval_jaxpr/top_k | solution.py:66
  461.0 6.6 %top_k.21 = (f32[256,256]{0,1:T(8,128)S(1)}, s32[256,256]{0,1:T(8,128)}) sort(f32[256,256]{0,1:T(8,128)S(1)} %copy.30, s32[256,256]{0,1:T(8,128)S(1)} %iota.11.clone.2), dimensions={1}, to_apply=%region_10.10 | sort | flops 1048576 | bytes 1048576 | tf_op jit(solution)/shard_map/while/body/eval_jaxpr/top_k | solution.py:66
  467.9 6.6 %top_k.21 = (f32[256,256]{0,1:T(8,128)S(1)}, s32[256,256]{0,1:T(8,128)}) sort(f32[256,256]{0,1:T(8,128)S(1)} %copy.30, s32[256,256]{0,1:T(8,128)S(1)} %iota.11.clone.2), dimensions={1}, to_apply=%region_10.10 | sort | flops 1048576 | bytes 1048576 | tf_op jit(solution)/shard_map/while/body/eval_jaxpr/top_k | solution.py:66
  474.9 6.6 %top_k.21 = (f32[256,256]{0,1:T(8,128)S(1)}, s32[256,256]{0,1:T(8,128)}) sort(f32[256,256]{0,1:T(8,128)S(1)} %copy.30, s32[256,256]{0,1:T(8,128)S(1)} %iota.11.clone.2), dimensions={1}, to_apply=%region_10.10 | sort | flops 1048576 | bytes 1048576 | tf_op jit(solution)/shard_map/while/body/eval_jaxpr/top_k | solution.py:66
  481.8 6.6 %top_k.21 = (f32[256,256]{0,1:T(8,128)S(1)}, s32[256,256]{0,1:T(8,128)}) sort(f32[256,256]{0,1:T(8,128)S(1)} %copy.30, s32[256,256]{0,1:T(8,128)S(1)} %iota.11.clone.2), dimensions={1}, to_apply=%region_10.10 | sort | flops 1048576 | bytes 1048576 | tf_op jit(solution)/shard_map/while/body/eval_jaxpr/top_k | solution.py:66
  488.8 6.6 %top_k.21 = (f32[256,256]{0,1:T(8,128)S(1)}, s32[256,256]{0,1:T(8,128)}) sort(f32[256,256]{0,1:T(8,128)S(1)} %copy.30, s32[256,256]{0,1:T(8,128)S(1)} %iota.11.clone.2), dimensions={1}, to_apply=%region_10.10 | sort | flops 1048576 | bytes 1048576 | tf_op jit(solution)/shard_map/while/body/eval_jaxpr/top_k | solution.py:66
  495.8 6.6 %top_k.21 = (f32[256,256]{0,1:T(8,128)S(1)}, s32[256,256]{0,1:T(8,128)}) sort(f32[256,256]{0,1:T(8,128)S(1)} %copy.30, s32[256,256]{0,1:T(8,128)S(1)} %iota.11.clone.2), dimensions={1}, to_apply=%region_10.10 | sort | flops 1048576 | bytes 1048576 | tf_op jit(solution)/shard_map/while/body/eval_jaxpr/top_k | solution.py:66
  502.7 6.6 %top_k.21 = (f32[256,256]{0,1:T(8,128)S(1)}, s32[256,256]{0,1:T(8,128)}) sort(f32[256,256]{0,1:T(8,128)S(1)} %copy.30, s32[256,256]{0,1:T(8,128)S(1)} %iota.11.clone.2), dimensions={1}, to_apply=%region_10.10 | sort | flops 1048576 | bytes 1048576 | tf_op jit(solution)/shard_map/while/body/eval_jaxpr/top_k | solution.py:66
  509.7 6.6 %top_k.21 = (f32[256,256]{0,1:T(8,128)S(1)}, s32[256,256]{0,1:T(8,128)}) sort(f32[256,256]{0,1:T(8,128)S(1)} %copy.30, s32[256,256]{0,1:T(8,128)S(1)} %iota.11.clone.2), dimensions={1}, to_apply=%region_10.10 | sort | flops 1048576 | bytes 1048576 | tf_op jit(solution)/shard_map/while/body/eval_jaxpr/top_k | solution.py:66
  516.6 6.6 %top_k.21 = (f32[256,256]{0,1:T(8,128)S(1)}, s32[256,256]{0,1:T(8,128)}) sort(f32[256,256]{0,1:T(8,128)S(1)} %copy.30, s32[256,256]{0,1:T(8,128)S(1)} %iota.11.clone.2), dimensions={1}, to_apply=%region_10.10 | sort | flops 1048576 | bytes 1048576 | tf_op jit(solution)/shard_map/while/body/eval_jaxpr/top_k | solution.py:66
  523.6 6.6 %top_k.21 = (f32[256,256]{0,1:T(8,128)S(1)}, s32[256,256]{0,1:T(8,128)}) sort(f32[256,256]{0,1:T(8,128)S(1)} %copy.30, s32[256,256]{0,1:T(8,128)S(1)} %iota.11.clone.2), dimensions={1}, to_apply=%region_10.10 | sort | flops 1048576 | bytes 1048576 | tf_op jit(solution)/shard_map/while/body/eval_jaxpr/top_k | solution.py:66
  (168 shorter events, 60.4 us)
Async XLA Ops:
  6.5 42.7 %all-gather.6.cloned.1.call-start = ((), (), s32[]{:S(2)}) async-start(), calls=%async_computation | async-start | bytes 1179648 | tf_op jit(solution)/shard_map/all_gather | solution.py:82
  9.3 89.9 %all-gather.8.cloned.1.call-start = ((), (), s32[]{:S(2)}) async-start(), calls=%async_computation.1 | async-start | bytes 1114112 | tf_op jit(solution)/shard_map/all_gather | solution.py:78
  11.9 411.5 %all-gather.10.cloned.1.call-start = ((), (), s32[]{:S(2)}) async-start(), calls=%async_computation.2 | async-start | bytes 2228224 | tf_op jit(solution)/shard_map/all_gather | solution.py:15
Sparse Core Ops, SparseCore 0:
  9.4 37.2 all-gather.5
  49.2 50.0 all-gather.7
  375.4 47.9 all-gather.9
where the time goes:
time: 541 us; the launch traced here: 537 us
  other arithmetic  176 us (33%)
  local copies, waits for them, and re-layouts  163 us (30%)
  waiting for transfers between devices  98.1 us (18%)
  matrix products  46.2 us (9%)
  blocking collectives  39.4 us (7%)
  between operations  13.9 us (3%)
    top_k x15, other arithmetic, keep_best(): lax.top_k(jnp.concatenate([first_list, second_list], axis=1), first_list....  98.5 us
    reshape x8, local copies, waits for them, and re-layouts, one_block(): similar = similar.reshape(row_count, query_tokens, block_width, doc_tokens)  79.4 us
    dot_general x8, local copies, waits for them, and re-layouts, one_block(): lax.dot_general(flat_queries, block_docs, (((1,), (1,)), ((), ())), prefe...  72 us
    reduce_max x8, other arithmetic, one_block(): return jnp.sum(jnp.max(similar, axis=3), axis=1).T  63.2 us
    all_gather x1, waiting for transfers between devices, body(): query_group = lax.all_gather(query_unit, 'doc', axis=0, tiled=True)  50 us
    all_gather x1, waiting for transfers between devices, joined(): pieces = lax.all_gather(value, axis)  48.1 us
    dot_general x8, matrix products, one_block(): lax.dot_general(flat_queries, block_docs, (((1,), (1,)), ((), ())), prefe...  46.2 us
    all_gather x1, blocking collectives, body(): group_lists = lax.all_gather(candidates, 'doc', axis=0, tiled=True)  19.4 us
  transfers between devices with their start and end apart: 3, of which 2 were waited for; matrix products, arithmetic and copies ran while one was open for 1% of the time, Pallas kernels for 0%

commit v1 on v0

v1 whole, which is shorter than its diff:
```python
import jax
import jax.numpy as jnp
from jax import lax
from jax.experimental import pallas as pl
from jax.experimental.pallas import tpu as pltpu
from jax.sharding import PartitionSpec as P

MESH = pl.DeviceIdType.MESH
epsilon = 1e-06
excluded_score = -1e30

OWN, UP1, DN1, UP2, DN2, UP3, DN3, FAR = range(8)
ZOFF = (0, 7, 2, 5, 1, 6, 3, 4)


def unit_rows(values):
    widened = values.astype(jnp.float32)
    return widened * lax.rsqrt(jnp.sum(widened * widened, axis=-1, keepdims=True) + epsilon)


def kernel(
    q_ref, d_ref, len_ref, cand_ref, o_ref,
    qstage, dstage, qbuf, dbuf, peaks, outbox, inbox, live, ranked,
    qsend, qrecv, dsend, drecv, csend, crecv, ssend, srecv,
):
    z = lax.axis_index("query")
    xy = lax.axis_index("doc")
    c = lax.axis_index("tok")
    x, y = xy // 4, xy % 4
    other = 1 - c

    def chip(dx, dy):
        return ((x + dx) % 4) * 4 + (y + dy) % 4

    barrier = pltpu.get_barrier_semaphore()

    def greet(n, carry):
        for tok in (0, 1):
            pl.semaphore_signal(
                barrier, inc=1, device_id={"doc": (xy + n) % 16, "tok": tok}, device_id_type=MESH
            )
        return carry

    for dz in (1, 7):
        pl.semaphore_signal(barrier, inc=1, device_id={"query": (z + dz) % 8}, device_id_type=MESH)
    pl.semaphore_signal(barrier, inc=1, device_id={"tok": other}, device_id_type=MESH)
    lax.fori_loop(1, 16, greet, 0)

    unit = unit_rows(q_ref[...]).reshape(256, 128)
    for n in range(16):
        qstage[pl.ds(n, 16, stride=16), :] = unit[n * 16:(n + 1) * 16]
    qbuf[0] = qstage[...].astype(jnp.bfloat16).reshape(2, 128, 128)
    slots = lax.broadcasted_iota(jnp.int32, (128, 128), 0)
    for w in range(4):
        unit = unit_rows(d_ref[w])
        unit = jnp.where(slots < len_ref[w], unit, unit[0:1])
        dstage[pl.ds(w, 128, stride=4), :] = unit
    dbuf[0] = dstage[...].astype(jnp.bfloat16).reshape(2, 256, 128)

    pl.semaphore_wait(barrier, 33)

    pending = []

    def q_copy(src, dst, sem, dx, dy):
        n = len([p for p in pending if p[0] == "q"])
        copy = pltpu.make_async_remote_copy(
            src_ref=src, dst_ref=dst, send_sem=qsend.at[n], recv_sem=sem,
            device_id={"doc": chip(dx, dy)}, device_id_type=MESH,
        )
        copy.start()
        pending.append(("q", copy))

    def q_whole(src, dst, dx, dy):
        q_copy(qbuf.at[src], qbuf.at[dst], qrecv.at[dst, 0], dx, dy)

    def q_half(h, src, dst, dx, dy):
        q_copy(qbuf.at[src, h], qbuf.at[dst, h], qrecv.at[dst, h], dx, dy)

    def q_wait(slot, h=None):
        ref = qbuf.at[slot] if h is None else qbuf.at[slot, h]
        pltpu.make_async_remote_copy(
            src_ref=ref, dst_ref=ref, send_sem=qsend.at[0], recv_sem=qrecv.at[slot, 0 if h is None else h],
            device_id={"doc": xy}, device_id_type=MESH,
        ).wait_recv()

    def z_copy(src, dst, part, dz):
        n = len([p for p in pending if p[0] == "d"])
        rows = pl.ds(0, 256) if part is None else pl.ds(part * 128, 128)
        copy = pltpu.make_async_remote_copy(
            src_ref=dbuf.at[src, c, rows], dst_ref=dbuf.at[dst, c, rows],
            send_sem=dsend.at[n], recv_sem=drecv.at[dst, 0 if part is None else part],
            device_id={"query": (z + dz) % 8}, device_id_type=MESH,
        )
        copy.start()
        pending.append(("d", copy))

    def z_wait(chunk, part=None):
        rows = pl.ds(0, 256) if part is None else pl.ds(part * 128, 128)
        ref = dbuf.at[chunk, c, rows]
        pltpu.make_async_remote_copy(
            src_ref=ref, dst_ref=ref, send_sem=dsend.at[0], recv_sem=drecv.at[chunk, 0 if part is None else part],
            device_id={"query": z}, device_id_type=MESH,
        ).wait_recv()

    def share(chunk):
        copy = pltpu.make_async_remote_copy(
            src_ref=dbuf.at[chunk, c], dst_ref=dbuf.at[chunk, c], send_sem=csend.at[chunk],
            recv_sem=crecv.at[chunk], device_id={"tok": other}, device_id_type=MESH,
        )
        copy.start()
        pending.append(("c", copy))

    def share_wait(chunk):
        ref = dbuf.at[chunk, other]
        pltpu.make_async_remote_copy(
            src_ref=ref, dst_ref=ref, send_sem=csend.at[0], recv_sem=crecv.at[chunk],
            device_id={"tok": c}, device_id_type=MESH,
        ).wait_recv()

    def match(slot, chunks):
        tokens = qbuf[slot].reshape(256, 128)
        for k in chunks:
            similar = lax.dot_general(
                dbuf[k].reshape(512, 128), tokens, (((1,), (1,)), ((), ())),
                preferred_element_type=jnp.float32,
            )
            peaks[slot, k] = jnp.max(similar.reshape(64, 8, 256), axis=0)

    sub = lax.broadcasted_iota(jnp.int32, (8, 128), 0)
    lane = lax.broadcasted_iota(jnp.int32, (8, 128), 1)

    def total(slot):
        pairs = []
        for p in range(4):
            both = 0.0
            for h in range(2):
                a = peaks[slot, 2 * p, :, h * 128:(h + 1) * 128]
                b = peaks[slot, 2 * p + 1, :, h * 128:(h + 1) * 128]
                first = jnp.where(sub < 4, a, b)
                second = jnp.where(sub < 4, b, a)
                both = both + jnp.maximum(first, pltpu.roll(second, 4, 0))
            pairs.append(both)
        low = lane < 64
        folded = []
        for p in (0, 2):
            a, b = pairs[p], pairs[p + 1]
            folded.append(jnp.where(low, a, b) + pltpu.roll(jnp.where(low, b, a), 64, 1))
        f0, f1 = folded
        quarter = jnp.where(lane % 64 < 32, f0 + pltpu.roll(f0, 96, 1), f1 + pltpu.roll(f1, 32, 1))
        even = quarter + pltpu.roll(quarter, 112, 1)
        odd = quarter + pltpu.roll(quarter, 16, 1)
        return jnp.where(lane % 32 < 16, even, pltpu.roll(odd, 4, 0))[0:4]

    def score_copy(slot, tok):
        return pltpu.make_async_remote_copy(
            src_ref=outbox.at[slot], dst_ref=inbox.at[c, slot], send_sem=ssend.at[slot, tok],
            recv_sem=srecv.at[c, slot],
            device_id={"doc": ((x - slot // 4 + 4) % 4) * 4 + (y - slot % 4 + 4) % 4, "tok": tok},
            device_id_type=MESH,
        )

    def deliver(slot):
        outbox[slot] = total(slot)
        score_copy(slot, 0).start()
        score_copy(slot, 1).start()

    q_whole(0, 4, 1, 0)
    q_whole(0, 12, 3, 0)
    q_whole(0, 1, 0, 1)
    q_whole(0, 3, 0, 3)
    z_copy(OWN, UP1, None, 1)
    z_copy(OWN, DN1, None, 7)

    rows = lax.broadcasted_iota(jnp.int32, (64, 256), 0)
    source = rows // 4
    row_id = (((x + source // 4) % 4) * 4 + (y + source % 4) % 4) * 4 + rows % 4
    lanes = lax.broadcasted_iota(jnp.int32, (128, 256), 0)
    group = lanes // 16
    plane = jnp.zeros_like(group)
    for g in range(8):
        plane = jnp.where(group == g, (z + ZOFF[g]) % 8, plane)
    first = cand_ref[0:1, :]
    second = cand_ref[1:2, :]
    listed = jnp.where(lanes % 16 < 8, first, second)
    by_plane = jnp.where(listed // 64 == plane, 1.0, 0.0).astype(jnp.bfloat16)
    found = []
    for block in (first, second):
        by_row = jnp.where(block % 64 == row_id, 1.0, 0.0).astype(jnp.bfloat16)
        found.append(lax.dot_general(
            by_row, by_plane, (((1,), (1,)), ((), ())), preferred_element_type=jnp.float32))
    wide_lane = lax.broadcasted_iota(jnp.int32, (64, 128), 1)
    live[...] = jnp.where(wide_lane % 16 < 8, found[0], found[1])

    match(0, (OWN,))

    near = (4, 12, 1, 3)
    q_wait(4)
    q_whole(4, 8, 1, 0)
    q_half(0, 4, 5, 0, 1)
    q_half(0, 4, 7, 0, 3)
    q_wait(12)
    q_half(0, 12, 13, 0, 1)
    q_half(0, 12, 15, 0, 3)
    q_wait(1)
    q_half(1, 1, 5, 1, 0)
    q_half(1, 1, 13, 3, 0)
    q_wait(3)
    q_whole(3, 2, 0, 3)
    q_half(1, 3, 7, 1, 0)
    q_half(1, 3, 15, 3, 0)
    z_wait(UP1)
    z_copy(UP1, UP2, None, 1)
    share(UP1)
    z_wait(DN1)
    z_copy(DN1, DN2, None, 7)
    share(DN1)

    for s in near:
        match(s, (OWN,))
    share_wait(UP1)
    share_wait(DN1)
    for s in (0,) + near:
        match(s, (UP1, DN1))

    q_wait(8)
    q_half(0, 8, 9, 0, 1)
    q_half(0, 8, 11, 0, 3)
    q_wait(2)
    q_half(1, 2, 6, 1, 0)
    q_half(1, 2, 14, 3, 0)
    for s in (5, 15, 7, 13):
        q_wait(s, 0)
        q_wait(s, 1)
    q_half(1, 5, 9, 1, 0)
    q_half(0, 5, 6, 0, 1)
    q_half(0, 15, 14, 0, 3)
    q_half(1, 15, 11, 3, 0)
    z_wait(UP2)
    z_copy(UP2, UP3, None, 1)
    share(UP2)
    z_wait(DN2)
    z_copy(DN2, DN3, None, 7)
    share(DN2)

    middle = (8, 2, 5, 7, 13, 15)
    for s in middle:
        match(s, (OWN, UP1, DN1))

    q_wait(9, 0)
    q_half(0, 9, 10, 0, 1)
    q_wait(14, 1)
    q_half(1, 14, 10, 3, 0)
    share_wait(UP2)
    share_wait(DN2)
    z_wait(UP3)
    z_copy(UP3, FAR, 0, 1)
    share(UP3)
    z_wait(DN3)
    z_copy(DN3, FAR, 1, 7)
    share(DN3)

    for s in (0,) + near + middle:
        match(s, (UP2, DN2))

    q_wait(9, 1)
    q_wait(14, 0)
    q_wait(6, 0)
    q_wait(6, 1)
    q_wait(11, 0)
    q_wait(11, 1)
    z_wait(FAR, 0)
    z_wait(FAR, 1)
    share(FAR)
    share_wait(UP3)
    share_wait(DN3)
    q_wait(10, 0)
    q_wait(10, 1)
    for s in (9, 14, 6, 11, 10):
        match(s, (OWN, UP1, DN1, UP2, DN2))
    share_wait(FAR)

    def last(n, carry):
        base = 12 - 4 * n
        for s in range(4):
            match(base + s, (UP3, DN3, FAR))
        for s in range(4):
            deliver(base + s)
        return carry

    lax.fori_loop(0, 3, last, 0)
    for s in range(4):
        match(s, (UP3, DN3, FAR))
    for s in (1, 2, 3):
        deliver(s)
    own = total(0)
    outbox[0] = own
    inbox[c, 0] = own
    sibling = pltpu.make_async_remote_copy(
        src_ref=outbox.at[0], dst_ref=inbox.at[c, 0], send_sem=ssend.at[0, 0], recv_sem=srecv.at[c, 0],
        device_id={"tok": other}, device_id_type=MESH,
    )
    sibling.start()

    for _, copy in pending:
        copy.wait_send()

    def arrive(tok, slot):
        ref = inbox.at[tok, slot]
        pltpu.make_async_remote_copy(
            src_ref=ref, dst_ref=ref, send_sem=ssend.at[0, 0], recv_sem=srecv.at[tok, slot],
            device_id={"tok": other}, device_id_type=MESH,
        ).wait_recv()

    def settle(slot, carry):
        arrive(0, slot)
        arrive(1, slot)
        score_copy(slot, 0).wait_send()
        score_copy(slot, 1).wait_send()
        return carry

    lax.fori_loop(1, 16, settle, 0)
    arrive(other, 0)
    sibling.wait_send()

    regs = []
    for v in range(8):
        pieces = [inbox[0, 2 * v + h] + inbox[1, 2 * v + h] for h in (0, 1)]
        value = jnp.concatenate(pieces, axis=0)
        regs.append(jnp.where(live[v * 8:(v + 1) * 8] > 0.0, value, excluded_score))

    def bit(k):
        return (sub >> (k - 3)) & 1 if k < 6 else (lane >> (k - 2)) & 1

    def partner(value, k):
        if k < 6:
            axis, step, size = 0, 1 << (k - 3), 8
        else:
            axis, step, size = 1, 1 << (k - 2), 128
        if 2 * step == size:
            return pltpu.roll(value, step, axis)
        return jnp.where(bit(k) == 0, pltpu.roll(value, size - step, axis), pltpu.roll(value, step, axis))

    def exchange(regs, k, flips=None):
        if k < 3:
            out = list(regs)
            for v in range(8):
                if v & (1 << k):
                    continue
                u = v | (1 << k)
                high, low = jnp.maximum(regs[v], regs[u]), jnp.minimum(regs[v], regs[u])
                if flips is not None and v & (1 << flips):
                    high, low = low, high
                out[v], out[u] = high, low
            return out
        keep_high = bit(k) == 0
        out = []
        for r in regs:
            mate = partner(r, k)
            out.append(jnp.where(keep_high, jnp.maximum(r, mate), jnp.minimum(r, mate)))
        return out

    def signed(regs, k):
        return [jnp.where(bit(k) == 0, r, -r) for r in regs]

    for phase in range(1, 10):
        top = min(phase - 1, 6)
        if phase in (8, 9):
            regs = [jnp.maximum(r, partner(r, phase - 1)) for r in regs]
        by_mask = 3 <= phase < 9
        if by_mask:
            regs = signed(regs, phase)
        for k in range(top, -1, -1):
            regs = exchange(regs, k, phase if phase < 3 else None)
        if by_mask:
            regs = signed(regs, phase)

    for v in range(8):
        ranked[pl.ds(v, 8, stride=8), :] = regs[v]
    turned = jnp.concatenate([ranked[...], ranked[...]], axis=0).T
    wide = lax.broadcasted_iota(jnp.int32, (16, 128), 1)
    o_ref[...] = jnp.where(wide < 64, turned[0:16], turned[16:32])


def body(queries, documents, doc_lengths, candidates):
    vmem = pl.BlockSpec(memory_space=pltpu.VMEM)
    return pl.pallas_call(
        kernel,
        out_shape=jax.ShapeDtypeStruct((16, 128), jnp.float32),
        in_specs=[vmem, vmem, pl.BlockSpec(memory_space=pltpu.SMEM), vmem],
        out_specs=vmem,
        scratch_shapes=[
            pltpu.VMEM((256, 128), jnp.float32),
            pltpu.VMEM((512, 128), jnp.float32),
            pltpu.VMEM((16, 2, 128, 128), jnp.bfloat16),
            pltpu.VMEM((8, 2, 256, 128), jnp.bfloat16),
            pltpu.VMEM((16, 8, 8, 256), jnp.float32),
            pltpu.VMEM((16, 4, 128), jnp.float32),
            pltpu.VMEM((2, 16, 4, 128), jnp.float32),
            pltpu.VMEM((64, 128), jnp.float32),
            pltpu.VMEM((64, 128), jnp.float32),
            pltpu.SemaphoreType.DMA((32,)),
            pltpu.SemaphoreType.DMA((16, 2)),
            pltpu.SemaphoreType.DMA((8,)),
            pltpu.SemaphoreType.DMA((8, 2)),
            pltpu.SemaphoreType.DMA((8,)),
            pltpu.SemaphoreType.DMA((8,)),
            pltpu.SemaphoreType.DMA((16, 2)),
            pltpu.SemaphoreType.DMA((2, 16)),
        ],
        compiler_params=pltpu.CompilerParams(
            collective_id=0, has_side_effects=True, vmem_limit_bytes=32 << 20
        ),
    )(queries, documents, doc_lengths, candidates)


def solution(mesh):
    in_specs = (
        P(("query", "doc"), "tok", None),
        P(("query", "doc"), None, None),
        P(("query", "doc")),
        P(("query", "doc"), None),
    )
    out_specs = P(("query", "doc"), None)
    return jax.shard_map(body, mesh=mesh, in_specs=in_specs, out_specs=out_specs, check_vma=False)
```

time: 541 us -> 45.3 us (0.08)
  other arithmetic: 176 us -> 0 us
  local copies, waits for them, and re-layouts: 163 us -> 3.68 us
  waiting for transfers between devices: 98.1 us -> 0 us
  matrix products: 46.2 us -> 0 us
  Pallas kernels: 0 us -> 41.5 us
  blocking collectives: 39.4 us -> 0 us
  between operations: 13.9 us -> 0.01 us
    top_k x16 -> x0, other arithmetic: 102 us -> none  [the longest x15 98.5 us: keep_best(): lax.top_k(jnp.concatenate([first_list, second_list], axis=1), first_list....]
    all_gather x3 -> x0, waiting for transfers between devices: 98.1 us -> none  [the longest x1 50 us: body(): query_group = lax.all_gather(query_unit, 'doc', axis=0, tiled=True)]
    reshape x11 -> x0, local copies, waits for them, and re-layouts: 79.6 us -> none  [the longest x8 79.4 us: one_block(): similar = similar.reshape(row_count, query_tokens, block_width, doc_tokens)]
    dot_general x8 -> x0, local copies, waits for them, and re-layouts: 72 us -> none  [one_block(): lax.dot_general(flat_queries, block_docs, (((1,), (1,)), ((), ())), prefe...]
    reduce_max x8 -> x0, other arithmetic: 63.2 us -> none  [one_block(): return jnp.sum(jnp.max(similar, axis=3), axis=1).T]
    dot_general x8 -> x0, matrix products: 46.2 us -> none  [one_block(): lax.dot_general(flat_queries, block_docs, (((1,), (1,)), ((), ())), prefe...]
    pallas_call x0 -> x1, Pallas kernels: none -> 41.5 us  [body(): pl.pallas_call(kernel, out_shape=jax.ShapeDtypeStruct((16, 128), jnp.floa...]
    all_gather x1 -> x0, blocking collectives: 19.4 us -> none  [body(): group_lists = lax.all_gather(candidates, 'doc', axis=0, tiled=True)]
  transfers between devices with their start and end apart: 3 -> 0, of which waited for: 2 -> 0; matrix products, arithmetic and copies ran while one was open for 1% -> 0% of each run, Pallas kernels for 0% -> 0%
where the time goes in v1:
time: 45.3 us; the launch traced here: 45.2 us
  Pallas kernels  41.5 us (92%)
  local copies, waits for them, and re-layouts  3.68 us (8%)
    pallas_call x1, Pallas kernels, body(): pl.pallas_call(kernel, out_shape=jax.ShapeDtypeStruct((16, 128), jnp.floa...  41.5 us
    unnamed x9, local copies, waits for them, and re-layouts  3.68 us

profile of v1, /device:TPU:1, one launch (start us, length us, event | category | flops | bytes accessed | tf_op | source)
XLA Modules:
  0.0 45.2 jit_solution(5610445973365192103)
XLA Ops:
  0.0 0.0 copy-start
  0.0 0.9 %copy-done = bf16[4,128,128]{2,1,0:T(8,128)(2,1)S(1)} copy-done((bf16[4,128,128]{2,1,0:T(8,128)(2,1)S(1)}, bf16[4,128,128]{2,1,0:T(8,128)(2,1)}, u32[]{:S(2)}) %copy-start) | copy-done | bytes 131096
  0.9 0.0 copy-start.1
  0.9 0.8 %copy-done.1 = bf16[16,16,128]{2,1,0:T(8,128)(2,1)S(1)} copy-done((bf16[16,16,128]{2,1,0:T(8,128)(2,1)S(1)}, bf16[16,16,128]{2,1,0:T(8,128)(2,1)}, u32[]{:S(2)}) %copy-start.1) | copy-done | bytes 65560
  1.7 0.0 copy-start.2
  1.7 0.7 %copy-done.2 = s32[2,256]{1,0:T(2,128)S(1)} copy-done((s32[2,256]{1,0:T(2,128)S(1)}, s32[2,256]{1,0:T(2,128)}, u32[]{:S(2)}) %copy-start.2) | copy-done | bytes 2072
  2.4 0.0 copy-start.3
  2.4 0.7 %copy-done.3 = s32[4]{0:T(128)S(1)} copy-done((s32[4]{0:T(128)S(1)}, s32[4]{0:T(128)}, u32[]{:S(2)}) %copy-start.3) | copy-done | bytes 40
  3.1 41.5 %shard_map.46 = f32[16,128]{1,0:T(8,128)S(1)} custom-call(bf16[16,16,128]{2,1,0:T(8,128)(2,1)S(1)} %copy-done.1, bf16[4,128,128]{2,1,0:T(8,128)(2,1)S(1)} %copy-done, s32[4]{0:T(128)S(1)} %copy-done.3, s32[2,256]{1,0:T(2,128)S(1)} %copy-done.2), custom_call_target="tpu_custom_call" | custom-call | tf_op jit(solution)/shard_map/pallas_call | solution.py:386
  44.6 0.6 %copy.6 = f32[16,128]{1,0:T(8,128)} copy(f32[16,128]{1,0:T(8,128)S(1)} %shard_map.46) | data formatting | bytes 16384
Async XLA Ops:
  0.0 0.9 %copy-start = (bf16[4,128,128]{2,1,0:T(8,128)(2,1)S(1)}, bf16[4,128,128]{2,1,0:T(8,128)(2,1)}, u32[]{:S(2)}) copy-start(bf16[4,128,128]{2,1,0:T(8,128)(2,1)} %d_ref.1) | copy-start | bytes 393220
  0.9 0.8 %copy-start.1 = (bf16[16,16,128]{2,1,0:T(8,128)(2,1)S(1)}, bf16[16,16,128]{2,1,0:T(8,128)(2,1)}, u32[]{:S(2)}) copy-start(bf16[16,16,128]{2,1,0:T(8,128)(2,1)} %q_ref.1) | copy-start | bytes 196612
  1.7 0.7 %copy-start.2 = (s32[2,256]{1,0:T(2,128)S(1)}, s32[2,256]{1,0:T(2,128)}, u32[]{:S(2)}) copy-start(s32[2,256]{1,0:T(2,128)} %cand_ref.1) | copy-start | bytes 6148
  2.4 0.7 %copy-start.3 = (s32[4]{0:T(128)S(1)}, s32[4]{0:T(128)}, u32[]{:S(2)}) copy-start(s32[4]{0:T(128)} %len_ref.1) | copy-start | bytes 52

commit v2 on v1

v2 whole, which is shorter than its diff:
```python
import jax
import jax.numpy as jnp
from jax import lax
from jax.experimental import pallas as pl
from jax.experimental.pallas import tpu as pltpu
from jax.sharding import PartitionSpec as P

MESH = pl.DeviceIdType.MESH
epsilon = 1e-06
excluded_score = -1e30

OWN, UP1, DN1, UP2, DN2, UP3, DN3, FAR = range(8)
ZOFF = (0, 7, 2, 5, 1, 6, 3, 4)


def unit_rows(values):
    widened = values.astype(jnp.float32)
    return widened * lax.rsqrt(jnp.sum(widened * widened, axis=-1, keepdims=True) + epsilon)


def kernel(
    q_hbm, d_hbm, len_hbm, cand_hbm, o_ref,
    q_ref, d_ref, len_ref, cand_ref, isem, qstage, dstage, qbuf, dbuf, peaks, outbox, inbox, live, ranked,
    qsend, qrecv, drecv, crecv, ssend, srecv,
):
    z = lax.axis_index("query")
    xy = lax.axis_index("doc")
    c = lax.axis_index("tok")
    x, y = xy // 4, xy % 4
    other = 1 - c

    def chip(dx, dy):
        return ((x + dx) % 4) * 4 + (y + dy) % 4

    near = (4, 12, 1, 3)
    axis = (8, 2)
    corner = (5, 7, 13, 15)
    far = (9, 11, 6, 14, 10)
    loads = [
        pltpu.make_async_copy(src, dst, isem.at[n])
        for n, (src, dst) in enumerate(
            ((q_hbm, q_ref), (d_hbm, d_ref), (len_hbm, len_ref), (cand_hbm, cand_ref)))
    ]
    for load in loads:
        load.start()

    barrier = pltpu.get_barrier_semaphore()

    def greet(**place):
        pl.semaphore_signal(barrier, inc=1, device_id=place, device_id_type=MESH)

    for dz in (1, 7, 2, 6):
        greet(query=(z + dz) % 8)
    for slot in near + axis + corner:
        greet(doc=chip(slot // 4, slot % 4))
    greet(tok=other)

    for load in loads:
        load.wait()

    unit = unit_rows(q_ref[...]).reshape(256, 128)
    for n in range(16):
        qstage[pl.ds(n, 16, stride=16), :] = unit[n * 16:(n + 1) * 16]
    qbuf[0] = qstage[...].astype(jnp.bfloat16).reshape(2, 128, 128)
    slots = lax.broadcasted_iota(jnp.int32, (128, 128), 0)
    for w in range(4):
        unit = unit_rows(d_ref[w])
        unit = jnp.where(slots < len_ref[w], unit, unit[0:1])
        dstage[pl.ds(w, 128, stride=4), :] = unit
    dbuf[0] = dstage[...].astype(jnp.bfloat16).reshape(2, 256, 128)

    pl.semaphore_wait(barrier, 15)

    pending = []

    def q_copy(ref_from, ref_to, recv, dx, dy):
        copy = pltpu.make_async_remote_copy(
            src_ref=ref_from, dst_ref=ref_to, send_sem=qsend.at[len(pending)], recv_sem=recv,
            device_id={"doc": chip(dx, dy)}, device_id_type=MESH,
        )
        copy.start()
        pending.append(copy)

    def q_send(slot):
        q_copy(qbuf.at[0], qbuf.at[slot], qrecv.at[slot, 0], slot // 4, slot % 4)

    def q_pass(half, slot, dx, dy):
        to = (slot // 4 + dx) % 4 * 4 + (slot % 4 + dy) % 4
        q_copy(qbuf.at[slot, half], qbuf.at[to, half], qrecv.at[to, half], dx, dy)

    def q_wait(slot, half=None):
        ref = qbuf.at[slot] if half is None else qbuf.at[slot, half]
        pltpu.make_async_remote_copy(
            src_ref=ref, dst_ref=ref, send_sem=qsend.at[0], recv_sem=qrecv.at[slot, half or 0],
            device_id={"doc": xy}, device_id_type=MESH,
        ).wait_recv()

    def z_copy(src, chunk, dz, part=None):
        rows = pl.ds(0, 256) if part is None else pl.ds(part * 128, 128)
        copy = pltpu.make_async_remote_copy(
            src_ref=dbuf.at[src, c, rows], dst_ref=dbuf.at[chunk, c, rows], send_sem=qsend.at[len(pending)],
            recv_sem=drecv.at[chunk, part or 0],
            device_id={"query": (z + dz) % 8}, device_id_type=MESH,
        )
        copy.start()
        pending.append(copy)

    def z_wait(chunk, part=None):
        rows = pl.ds(0, 256) if part is None else pl.ds(part * 128, 128)
        ref = dbuf.at[chunk, c, rows]
        pltpu.make_async_remote_copy(
            src_ref=ref, dst_ref=ref, send_sem=qsend.at[0], recv_sem=drecv.at[chunk, part or 0],
            device_id={"query": z}, device_id_type=MESH,
        ).wait_recv()

    def share(chunk):
        copy = pltpu.make_async_remote_copy(
            src_ref=dbuf.at[chunk, c], dst_ref=dbuf.at[chunk, c], send_sem=qsend.at[len(pending)],
            recv_sem=crecv.at[chunk], device_id={"tok": other}, device_id_type=MESH,
        )
        copy.start()
        pending.append(copy)

    def share_wait(chunk):
        ref = dbuf.at[chunk, other]
        pltpu.make_async_remote_copy(
            src_ref=ref, dst_ref=ref, send_sem=qsend.at[0], recv_sem=crecv.at[chunk],
            device_id={"tok": c}, device_id_type=MESH,
        ).wait_recv()

    def match(slot, chunks):
        tokens = qbuf[slot].reshape(256, 128)
        for k in chunks:
            similar = lax.dot_general(
                dbuf[k].reshape(512, 128), tokens, (((1,), (1,)), ((), ())),
                preferred_element_type=jnp.float32,
            )
            peaks[slot, k] = jnp.max(similar.reshape(64, 8, 256), axis=0)

    sub = lax.broadcasted_iota(jnp.int32, (8, 128), 0)
    lane = lax.broadcasted_iota(jnp.int32, (8, 128), 1)

    def total(slot):
        pairs = []
        for p in range(4):
            both = 0.0
            for h in range(2):
                a = peaks[slot, 2 * p, :, h * 128:(h + 1) * 128]
                b = peaks[slot, 2 * p + 1, :, h * 128:(h + 1) * 128]
                first = jnp.where(sub < 4, a, b)
                second = jnp.where(sub < 4, b, a)
                both = both + jnp.maximum(first, pltpu.roll(second, 4, 0))
            pairs.append(both)
        low = lane < 64
        folded = []
        for p in (0, 2):
            a, b = pairs[p], pairs[p + 1]
            folded.append(jnp.where(low, a, b) + pltpu.roll(jnp.where(low, b, a), 64, 1))
        f0, f1 = folded
        quarter = jnp.where((lane & 63) < 32, f0 + pltpu.roll(f0, 96, 1), f1 + pltpu.roll(f1, 32, 1))
        even = quarter + pltpu.roll(quarter, 112, 1)
        odd = quarter + pltpu.roll(quarter, 16, 1)
        return jnp.where((lane & 31) < 16, even, pltpu.roll(odd, 4, 0))[0:4]

    def score_copy(slot, tok):
        return pltpu.make_async_remote_copy(
            src_ref=outbox.at[slot], dst_ref=inbox.at[c, slot], send_sem=ssend.at[slot, tok],
            recv_sem=srecv.at[c, slot],
            device_id={"doc": ((x - slot // 4 + 4) % 4) * 4 + (y - slot % 4 + 4) % 4, "tok": tok},
            device_id_type=MESH,
        )

    z_copy(OWN, UP1, 1)
    z_copy(OWN, DN1, 7)
    for slot in near:
        q_send(slot)
    z_copy(OWN, UP2, 2)
    z_copy(OWN, DN2, 6)
    for slot in axis:
        q_send(slot)
    for slot in corner:
        q_send(slot)

    rows = lax.broadcasted_iota(jnp.int32, (64, 256), 0)
    source = rows >> 2
    row_id = (((x + (source >> 2)) & 3) * 4 + ((y + source) & 3)) * 4 + (rows & 3)
    lanes = lax.broadcasted_iota(jnp.int32, (128, 256), 0)
    group = lanes >> 4
    plane = jnp.zeros_like(group)
    for g in range(8):
        plane = jnp.where(group == g, (z + ZOFF[g]) % 8, plane)
    first = cand_ref[0:1, :]
    second = cand_ref[1:2, :]
    listed = jnp.where((lanes & 15) < 8, first, second)
    by_plane = jnp.where(listed >> 6 == plane, 1.0, 0.0).astype(jnp.bfloat16)
    found = []
    for block in (first, second):
        by_row = jnp.where(block & 63 == row_id, 1.0, 0.0).astype(jnp.bfloat16)
        found.append(lax.dot_general(
            by_row, by_plane, (((1,), (1,)), ((), ())), preferred_element_type=jnp.float32))
    wide_lane = lax.broadcasted_iota(jnp.int32, (64, 128), 1)
    live[...] = jnp.where((wide_lane & 15) < 8, found[0], found[1])

    match(0, (OWN,))

    for s in near:
        q_wait(s)
    q_pass(1, 1, 2, 0)
    q_pass(1, 3, 2, 0)
    q_pass(0, 4, 0, 2)
    q_pass(0, 12, 0, 2)
    z_wait(UP1)
    share(UP1)
    z_copy(UP1, UP3, 2)
    z_wait(DN1)
    share(DN1)
    z_copy(DN1, DN3, 6)
    for s in near:
        match(s, (OWN,))
    share_wait(UP1)
    share_wait(DN1)
    for s in (0,) + near:
        match(s, (UP1, DN1))

    q_wait(8)
    q_wait(2)
    for d in (1, 3, 2):
        q_pass(0, 8, 0, d)
        q_pass(1, 2, d, 0)
    z_wait(UP2)
    z_copy(UP2, FAR, 2, 0)
    share(UP2)
    z_wait(DN2)
    z_copy(DN2, FAR, 6, 1)
    share(DN2)
    for s in axis:
        match(s, (OWN, UP1, DN1))
    share_wait(UP2)
    share_wait(DN2)
    for s in (0,) + near + axis:
        match(s, (UP2, DN2))

    for s in corner:
        q_wait(s)
    for s in corner:
        match(s, (OWN, UP1, DN1, UP2, DN2))

    z_wait(UP3)
    share(UP3)
    z_wait(DN3)
    share(DN3)
    for s in far:
        q_wait(s, 0)
        q_wait(s, 1)
    for s in far:
        match(s, (OWN, UP1, DN1, UP2, DN2))
    z_wait(FAR, 0)
    z_wait(FAR, 1)
    share(FAR)
    share_wait(UP3)
    share_wait(DN3)
    for s in far + corner + axis + near + (0,):
        match(s, (UP3, DN3))
    share_wait(FAR)

    def deliver(slots):
        for s in slots:
            if s:
                score_copy(s, 0).start()
                score_copy(s, 1).start()

    waves = (far, corner, axis + near[:2], near[2:] + (0,))
    for n, wave in enumerate(waves):
        for s in wave:
            match(s, (FAR,))
        if n:
            for s in waves[n - 1]:
                outbox[s] = total(s)
            deliver(waves[n - 1])
    sums = [total(s) for s in waves[-1]]
    for s, value in zip(waves[-1], sums):
        outbox[s] = value
    inbox[c, 0] = sums[-1]
    deliver(waves[-1])
    sibling = pltpu.make_async_remote_copy(
        src_ref=outbox.at[0], dst_ref=inbox.at[c, 0], send_sem=ssend.at[0, 0], recv_sem=srecv.at[c, 0],
        device_id={"tok": other}, device_id_type=MESH,
    )
    sibling.start()

    def arrive(tok, slot):
        ref = inbox.at[tok, slot]
        pltpu.make_async_remote_copy(
            src_ref=ref, dst_ref=ref, send_sem=ssend.at[0, 0], recv_sem=srecv.at[tok, slot],
            device_id={"tok": other}, device_id_type=MESH,
        ).wait_recv()

    arrive(other, 0)
    for slot in range(1, 16):
        arrive(0, slot)
        arrive(1, slot)

    regs = []
    for v in range(8):
        pieces = [inbox[0, 2 * v + h] + inbox[1, 2 * v + h] for h in (0, 1)]
        value = jnp.concatenate(pieces, axis=0)
        regs.append(jnp.where(live[v * 8:(v + 1) * 8] > 0.0, value, excluded_score))

    def bit(k):
        return (sub >> (k - 3)) & 1 if k < 6 else (lane >> (k - 2)) & 1

    def partner(value, k):
        if k < 6:
            axis, step, size = 0, 1 << (k - 3), 8
        else:
            axis, step, size = 1, 1 << (k - 2), 128
        if 2 * step == size:
            return pltpu.roll(value, step, axis)
        return jnp.where(bit(k) == 0, pltpu.roll(value, size - step, axis), pltpu.roll(value, step, axis))

    def exchange(regs, k, flips=None):
        if k < 3:
            out = list(regs)
            for v in range(8):
                if v & (1 << k):
                    continue
                u = v | (1 << k)
                high, low = jnp.maximum(regs[v], regs[u]), jnp.minimum(regs[v], regs[u])
                if flips is not None and v & (1 << flips):
                    high, low = low, high
                out[v], out[u] = high, low
            return out
        keep_high = bit(k) == 0
        out = []
        for r in regs:
            mate = partner(r, k)
            out.append(jnp.where(keep_high, jnp.maximum(r, mate), jnp.minimum(r, mate)))
        return out

    def signed(regs, k):
        return [jnp.where(bit(k) == 0, r, -r) for r in regs]

    for phase in range(1, 10):
        top = min(phase - 1, 6)
        if phase in (8, 9):
            regs = [jnp.maximum(r, partner(r, phase - 1)) for r in regs]
        by_mask = 3 <= phase < 9
        if by_mask:
            regs = signed(regs, phase)
        for k in range(top, -1, -1):
            regs = exchange(regs, k, phase if phase < 3 else None)
        if by_mask:
            regs = signed(regs, phase)

    for v in range(8):
        ranked[pl.ds(v, 8, stride=8), :] = regs[v]
    turned = jnp.concatenate([ranked[...], ranked[...]], axis=0).T
    wide = lax.broadcasted_iota(jnp.int32, (16, 128), 1)
    o_ref[...] = jnp.where(wide < 64, turned[0:16], turned[16:32])

    for copy in pending:
        copy.wait_send()
    for slot in range(1, 16):
        score_copy(slot, 0).wait_send()
        score_copy(slot, 1).wait_send()
    sibling.wait_send()


def body(queries, documents, doc_lengths, candidates):
    vmem = pl.BlockSpec(memory_space=pltpu.VMEM)
    return pl.pallas_call(
        kernel,
        out_shape=jax.ShapeDtypeStruct((16, 128), jnp.float32),
        in_specs=[pl.BlockSpec(memory_space=pltpu.HBM)] * 4,
        out_specs=vmem,
        scratch_shapes=[
            pltpu.VMEM((16, 16, 128), jnp.bfloat16),
            pltpu.VMEM((4, 128, 128), jnp.bfloat16),
            pltpu.SMEM((4,), jnp.int32),
            pltpu.VMEM((2, 256), jnp.int32),
            pltpu.SemaphoreType.DMA((4,)),
            pltpu.VMEM((256, 128), jnp.float32),
            pltpu.VMEM((512, 128), jnp.float32),
            pltpu.VMEM((16, 2, 128, 128), jnp.bfloat16),
            pltpu.VMEM((8, 2, 256, 128), jnp.bfloat16),
            pltpu.VMEM((16, 8, 8, 256), jnp.float32),
            pltpu.VMEM((16, 4, 128), jnp.float32),
            pltpu.VMEM((2, 16, 4, 128), jnp.float32),
            pltpu.VMEM((64, 128), jnp.float32),
            pltpu.VMEM((64, 128), jnp.float32),
            pltpu.SemaphoreType.DMA((40,)),
            pltpu.SemaphoreType.DMA((16, 2)),
            pltpu.SemaphoreType.DMA((8, 2)),
            pltpu.SemaphoreType.DMA((8,)),
            pltpu.SemaphoreType.DMA((16, 2)),
            pltpu.SemaphoreType.DMA((2, 16)),
        ],
        compiler_params=pltpu.CompilerParams(
            collective_id=0, has_side_effects=True, vmem_limit_bytes=60 << 20
        ),
    )(queries, documents, doc_lengths, candidates)


def solution(mesh):
    in_specs = (
        P(("query", "doc"), "tok", None),
        P(("query", "doc"), None, None),
        P(("query", "doc")),
        P(("query", "doc"), None),
    )
    out_specs = P(("query", "doc"), None)
    return jax.shard_map(body, mesh=mesh, in_specs=in_specs, out_specs=out_specs, check_vma=False)
```

time: 45.3 us -> 38 us (0.84)
  Pallas kernels: 41.5 us -> 36.6 us
  local copies, waits for them, and re-layouts: 3.68 us -> 1.3 us
    pallas_call x1, Pallas kernels: 41.5 us -> 36.6 us  [body(): pl.pallas_call(kernel, out_shape=jax.ShapeDtypeStruct((16, 128), jnp.floa...]
    unnamed x9 -> x1, local copies, waits for them, and re-layouts: 3.68 us -> 1.3 us
where the time goes in v2:
time: 38 us; the launch traced here: 37.9 us
  Pallas kernels  36.6 us (96%)
  local copies, waits for them, and re-layouts  1.3 us (3%)
    pallas_call x1, Pallas kernels, body(): pl.pallas_call(kernel, out_shape=jax.ShapeDtypeStruct((16, 128), jnp.floa...  36.6 us
    unnamed x1, local copies, waits for them, and re-layouts  1.3 us

profile of v2, /device:TPU:1, one launch (start us, length us, event | category | flops | bytes accessed | tf_op | source)
XLA Modules:
  0.0 37.9 jit_solution(2631971003459157071)
XLA Ops:
  0.0 36.6 %shard_map.46 = f32[16,128]{1,0:T(8,128)} custom-call(bf16[16,16,128]{2,1,0:T(8,128)(2,1)} %q_hbm.1, bf16[4,128,128]{2,1,0:T(8,128)(2,1)} %d_hbm.1, s32[4]{0:T(128)} %len_hbm.1, s32[2,256]{1,0:T(2,128)} %cand_hbm.1), custom_call_target="tpu_custom_call" | custom-call | tf_op jit(solution)/shard_map/pallas_call | solution.py:371
  36.6 1.3 %copy.6 = f32[16,128]{1,0:T(8,128)} copy(f32[16,128]{1,0:T(8,128)} %shard_map.46) | data formatting | bytes 16384

commit v3 on v2

--- a/solution.py
+++ b/solution.py
@@ -51,7 +51,7 @@
 
     for dz in (1, 7, 2, 6):
         greet(query=(z + dz) % 8)
-    for slot in near + axis + corner:
+    for slot in near + axis:
         greet(doc=chip(slot // 4, slot % 4))
     greet(tok=other)
 
@@ -67,9 +67,9 @@
         unit = unit_rows(d_ref[w])
         unit = jnp.where(slots < len_ref[w], unit, unit[0:1])
         dstage[pl.ds(w, 128, stride=4), :] = unit
-    dbuf[0] = dstage[...].astype(jnp.bfloat16).reshape(2, 256, 128)
-
-    pl.semaphore_wait(barrier, 15)
+    dbuf[:, OWN] = dstage[...].astype(jnp.bfloat16).reshape(2, 256, 128)
+
+    pl.semaphore_wait(barrier, 11)
 
     pending = []
 
@@ -98,7 +98,7 @@
     def z_copy(src, chunk, dz, part=None):
         rows = pl.ds(0, 256) if part is None else pl.ds(part * 128, 128)
         copy = pltpu.make_async_remote_copy(
-            src_ref=dbuf.at[src, c, rows], dst_ref=dbuf.at[chunk, c, rows], send_sem=qsend.at[len(pending)],
+            src_ref=dbuf.at[c, src, rows], dst_ref=dbuf.at[c, chunk, rows], send_sem=qsend.at[len(pending)],
             recv_sem=drecv.at[chunk, part or 0],
             device_id={"query": (z + dz) % 8}, device_id_type=MESH,
         )
@@ -107,7 +107,7 @@
 
     def z_wait(chunk, part=None):
         rows = pl.ds(0, 256) if part is None else pl.ds(part * 128, 128)
-        ref = dbuf.at[chunk, c, rows]
+        ref = dbuf.at[c, chunk, rows]
         pltpu.make_async_remote_copy(
             src_ref=ref, dst_ref=ref, send_sem=qsend.at[0], recv_sem=drecv.at[chunk, part or 0],
             device_id={"query": z}, device_id_type=MESH,
@@ -115,27 +115,31 @@
 
     def share(chunk):
         copy = pltpu.make_async_remote_copy(
-            src_ref=dbuf.at[chunk, c], dst_ref=dbuf.at[chunk, c], send_sem=qsend.at[len(pending)],
+            src_ref=dbuf.at[c, chunk], dst_ref=dbuf.at[c, chunk], send_sem=qsend.at[len(pending)],
             recv_sem=crecv.at[chunk], device_id={"tok": other}, device_id_type=MESH,
         )
         copy.start()
         pending.append(copy)
 
     def share_wait(chunk):
-        ref = dbuf.at[chunk, other]
+        ref = dbuf.at[other, chunk]
         pltpu.make_async_remote_copy(
             src_ref=ref, dst_ref=ref, send_sem=qsend.at[0], recv_sem=crecv.at[chunk],
             device_id={"tok": c}, device_id_type=MESH,
         ).wait_recv()
 
-    def match(slot, chunks):
-        tokens = qbuf[slot].reshape(256, 128)
-        for k in chunks:
-            similar = lax.dot_general(
-                dbuf[k].reshape(512, 128), tokens, (((1,), (1,)), ((), ())),
-                preferred_element_type=jnp.float32,
-            )
-            peaks[slot, k] = jnp.max(similar.reshape(64, 8, 256), axis=0)
+    def match(slots, start, count, halves):
+        for half in halves:
+            joins = half is other
+            for slot in slots:
+                similar = lax.dot_general(
+                    dbuf[half, start:start + count].reshape(count * 256, 128), qbuf[slot].reshape(256, 128),
+                    (((1,), (1,)), ((), ())), preferred_element_type=jnp.float32,
+                )
+                best = jnp.max(similar.reshape(count, 32, 8, 256), axis=1)
+                if joins:
+                    best = jnp.maximum(best, peaks[slot, start:start + count])
+                peaks[slot, start:start + count] = best
 
     sub = lax.broadcasted_iota(jnp.int32, (8, 128), 0)
     lane = lax.broadcasted_iota(jnp.int32, (8, 128), 1)
@@ -170,16 +174,18 @@
             device_id_type=MESH,
         )
 
+    z_copy(OWN, UP2, 2, 0)
+    z_copy(OWN, DN2, 6, 1)
+    for slot in near[:2]:
+        q_send(slot)
     z_copy(OWN, UP1, 1)
     z_copy(OWN, DN1, 7)
-    for slot in near:
+    for slot in near[2:]:
         q_send(slot)
-    z_copy(OWN, UP2, 2)
-    z_copy(OWN, DN2, 6)
     for slot in axis:
         q_send(slot)
-    for slot in corner:
-        q_send(slot)
+    z_copy(OWN, UP2, 2, 1)
+    z_copy(OWN, DN2, 6, 0)
 
     rows = lax.broadcasted_iota(jnp.int32, (64, 256), 0)
     source = rows >> 2
@@ -201,66 +207,82 @@
     wide_lane = lax.broadcasted_iota(jnp.int32, (64, 128), 1)
     live[...] = jnp.where((wide_lane & 15) < 8, found[0], found[1])
 
-    match(0, (OWN,))
-
-    for s in near:
-        q_wait(s)
+    both = (c, other)
+    match((0,), OWN, 1, both)
+
+    q_wait(4)
+    q_pass(0, 4, 0, 1)
+    q_pass(0, 4, 0, 3)
+    q_wait(12)
+    q_pass(0, 12, 0, 1)
+    q_pass(0, 12, 0, 3)
+    q_wait(1)
+    q_pass(1, 1, 1, 0)
+    q_pass(1, 1, 3, 0)
+    q_wait(3)
+    q_pass(1, 3, 1, 0)
+    q_pass(1, 3, 3, 0)
+    z_wait(UP2, 0)
+    z_copy(UP2, FAR, 2, 0)
+    z_copy(UP2, UP3, 1, 0)
+    z_wait(DN2, 1)
+    z_copy(DN2, FAR, 6, 1)
+    z_copy(DN2, DN3, 7, 1)
+    z_wait(UP1)
+    share(UP1)
+    z_wait(DN1)
+    share(DN1)
+    q_pass(0, 4, 0, 2)
+    q_pass(0, 12, 0, 2)
     q_pass(1, 1, 2, 0)
     q_pass(1, 3, 2, 0)
-    q_pass(0, 4, 0, 2)
-    q_pass(0, 12, 0, 2)
-    z_wait(UP1)
-    share(UP1)
-    z_copy(UP1, UP3, 2)
-    z_wait(DN1)
-    share(DN1)
-    z_copy(DN1, DN3, 6)
-    for s in near:
-        match(s, (OWN,))
-    share_wait(UP1)
-    share_wait(DN1)
-    for s in (0,) + near:
-        match(s, (UP1, DN1))
-
+    match(near, OWN, 1, both)
     q_wait(8)
     q_wait(2)
     for d in (1, 3, 2):
         q_pass(0, 8, 0, d)
         q_pass(1, 2, d, 0)
-    z_wait(UP2)
-    z_copy(UP2, FAR, 2, 0)
+    inner = (0,) + near + axis
+    match(inner, UP1, 2, (c,))
+    z_wait(UP2, 1)
+    z_copy(UP2, UP3, 1, 1)
     share(UP2)
-    z_wait(DN2)
-    z_copy(DN2, FAR, 6, 1)
+    z_wait(DN2, 0)
+    z_copy(DN2, DN3, 7, 0)
     share(DN2)
-    for s in axis:
-        match(s, (OWN, UP1, DN1))
+    match(axis, OWN, 1, both)
+    share_wait(UP1)
+    share_wait(DN1)
+    match(inner, UP1, 2, (other,))
+    match(inner, UP2, 2, (c,))
     share_wait(UP2)
     share_wait(DN2)
-    for s in (0,) + near + axis:
-        match(s, (UP2, DN2))
+    match(inner, UP2, 2, (other,))
 
     for s in corner:
-        q_wait(s)
-    for s in corner:
-        match(s, (OWN, UP1, DN1, UP2, DN2))
-
-    z_wait(UP3)
-    share(UP3)
-    z_wait(DN3)
-    share(DN3)
-    for s in far:
         q_wait(s, 0)
         q_wait(s, 1)
-    for s in far:
-        match(s, (OWN, UP1, DN1, UP2, DN2))
+        match((s,), OWN, 5, both)
+    for part in (0, 1):
+        z_wait(UP3, part)
+    share(UP3)
+    for part in (1, 0):
+        z_wait(DN3, part)
+    share(DN3)
+    for s in far[:2]:
+        q_wait(s, 0)
+        q_wait(s, 1)
+        match((s,), OWN, 5, both)
     z_wait(FAR, 0)
     z_wait(FAR, 1)
     share(FAR)
+    for s in far[2:]:
+        q_wait(s, 0)
+        q_wait(s, 1)
+        match((s,), OWN, 5, both)
+    match(range(16), UP3, 3, (c,))
     share_wait(UP3)
     share_wait(DN3)
-    for s in far + corner + axis + near + (0,):
-        match(s, (UP3, DN3))
     share_wait(FAR)
 
     def deliver(slots):
@@ -271,8 +293,7 @@
 
     waves = (far, corner, axis + near[:2], near[2:] + (0,))
     for n, wave in enumerate(waves):
-        for s in wave:
-            match(s, (FAR,))
+        match(wave, UP3, 3, (other,))
         if n:
             for s in waves[n - 1]:
                 outbox[s] = total(s)
@@ -382,13 +403,13 @@
             pltpu.VMEM((256, 128), jnp.float32),
             pltpu.VMEM((512, 128), jnp.float32),
             pltpu.VMEM((16, 2, 128, 128), jnp.bfloat16),
-            pltpu.VMEM((8, 2, 256, 128), jnp.bfloat16),
+            pltpu.VMEM((2, 8, 256, 128), jnp.bfloat16),
             pltpu.VMEM((16, 8, 8, 256), jnp.float32),
             pltpu.VMEM((16, 4, 128), jnp.float32),
             pltpu.VMEM((2, 16, 4, 128), jnp.float32),
             pltpu.VMEM((64, 128), jnp.float32),
             pltpu.VMEM((64, 128), jnp.float32),
-            pltpu.SemaphoreType.DMA((40,)),
+            pltpu.SemaphoreType.DMA((48,)),
             pltpu.SemaphoreType.DMA((16, 2)),
             pltpu.SemaphoreType.DMA((8, 2)),
             pltpu.SemaphoreType.DMA((8,)),

time: 38 us -> 35.8 us (0.942)
  Pallas kernels: 36.6 us -> 34.4 us
    pallas_call x1, Pallas kernels: 36.6 us -> 34.4 us  [body(): pl.pallas_call(kernel, out_shape=jax.ShapeDtypeStruct((16, 128), jnp.floa...]
where the time goes in v3:
time: 35.8 us; the launch traced here: 35.7 us
  Pallas kernels  34.4 us (96%)
  local copies, waits for them, and re-layouts  1.3 us (4%)
    pallas_call x1, Pallas kernels, body(): pl.pallas_call(kernel, out_shape=jax.ShapeDtypeStruct((16, 128), jnp.floa...  34.4 us
    unnamed x1, local copies, waits for them, and re-layouts  1.3 us

profile of v3, /device:TPU:1, one launch (start us, length us, event | category | flops | bytes accessed | tf_op | source)
XLA Modules:
  0.0 35.7 jit_solution(8879745849680884657)
XLA Ops:
  0.0 34.4 %shard_map.46 = f32[16,128]{1,0:T(8,128)} custom-call(bf16[16,16,128]{2,1,0:T(8,128)(2,1)} %q_hbm.1, bf16[4,128,128]{2,1,0:T(8,128)(2,1)} %d_hbm.1, s32[4]{0:T(128)} %len_hbm.1, s32[2,256]{1,0:T(2,128)} %cand_hbm.1), custom_call_target="tpu_custom_call" | custom-call | tf_op jit(solution)/shard_map/pallas_call | solution.py:392
  34.4 1.3 %copy.6 = f32[16,128]{1,0:T(8,128)} copy(f32[16,128]{1,0:T(8,128)} %shard_map.46) | data formatting | bytes 16384

commit v4 on v3

--- a/solution.py
+++ b/solution.py
@@ -39,7 +39,7 @@
     loads = [
         pltpu.make_async_copy(src, dst, isem.at[n])
         for n, (src, dst) in enumerate(
-            ((q_hbm, q_ref), (d_hbm, d_ref), (len_hbm, len_ref), (cand_hbm, cand_ref)))
+            ((d_hbm, d_ref), (len_hbm, len_ref), (q_hbm, q_ref), (cand_hbm, cand_ref)))
     ]
     for load in loads:
         load.start()
@@ -55,13 +55,8 @@
         greet(doc=chip(slot // 4, slot % 4))
     greet(tok=other)
 
-    for load in loads:
-        load.wait()
-
-    unit = unit_rows(q_ref[...]).reshape(256, 128)
-    for n in range(16):
-        qstage[pl.ds(n, 16, stride=16), :] = unit[n * 16:(n + 1) * 16]
-    qbuf[0] = qstage[...].astype(jnp.bfloat16).reshape(2, 128, 128)
+    loads[0].wait()
+    loads[1].wait()
     slots = lax.broadcasted_iota(jnp.int32, (128, 128), 0)
     for w in range(4):
         unit = unit_rows(d_ref[w])
@@ -176,16 +171,19 @@
 
     z_copy(OWN, UP2, 2, 0)
     z_copy(OWN, DN2, 6, 1)
-    for slot in near[:2]:
-        q_send(slot)
     z_copy(OWN, UP1, 1)
     z_copy(OWN, DN1, 7)
-    for slot in near[2:]:
-        q_send(slot)
-    for slot in axis:
+
+    loads[2].wait()
+    unit = unit_rows(q_ref[...]).reshape(256, 128)
+    for n in range(16):
+        qstage[pl.ds(n, 16, stride=16), :] = unit[n * 16:(n + 1) * 16]
+    qbuf[0] = qstage[...].astype(jnp.bfloat16).reshape(2, 128, 128)
+    for slot in near + axis:
         q_send(slot)
     z_copy(OWN, UP2, 2, 1)
     z_copy(OWN, DN2, 6, 0)
+    loads[3].wait()
 
     rows = lax.broadcasted_iota(jnp.int32, (64, 256), 0)
     source = rows >> 2
@@ -236,13 +234,13 @@
     q_pass(0, 12, 0, 2)
     q_pass(1, 1, 2, 0)
     q_pass(1, 3, 2, 0)
-    match(near, OWN, 1, both)
     q_wait(8)
     q_wait(2)
     for d in (1, 3, 2):
         q_pass(0, 8, 0, d)
         q_pass(1, 2, d, 0)
-    inner = (0,) + near + axis
+    match(near, OWN, 1, both)
+    inner = near + axis
     match(inner, UP1, 2, (c,))
     z_wait(UP2, 1)
     z_copy(UP2, UP3, 1, 1)
@@ -251,18 +249,17 @@
     z_copy(DN2, DN3, 7, 0)
     share(DN2)
     match(axis, OWN, 1, both)
+    match(inner, UP2, 2, (c,))
     share_wait(UP1)
     share_wait(DN1)
-    match(inner, UP1, 2, (other,))
-    match(inner, UP2, 2, (c,))
     share_wait(UP2)
     share_wait(DN2)
-    match(inner, UP2, 2, (other,))
+    match(inner, UP1, 4, (other,))
 
     for s in corner:
         q_wait(s, 0)
         q_wait(s, 1)
-        match((s,), OWN, 5, both)
+    match(corner, OWN, 5, both)
     for part in (0, 1):
         z_wait(UP3, part)
     share(UP3)
@@ -272,15 +269,14 @@
     for s in far[:2]:
         q_wait(s, 0)
         q_wait(s, 1)
-        match((s,), OWN, 5, both)
     z_wait(FAR, 0)
     z_wait(FAR, 1)
     share(FAR)
     for s in far[2:]:
         q_wait(s, 0)
         q_wait(s, 1)
-        match((s,), OWN, 5, both)
-    match(range(16), UP3, 3, (c,))
+    match(far, OWN, 5, both)
+    match(range(1, 16), UP3, 3, (c,))
     share_wait(UP3)
     share_wait(DN3)
     share_wait(FAR)
@@ -291,18 +287,24 @@
                 score_copy(s, 0).start()
                 score_copy(s, 1).start()
 
-    waves = (far, corner, axis + near[:2], near[2:] + (0,))
+    waves = (far, corner, axis, near)
     for n, wave in enumerate(waves):
         match(wave, UP3, 3, (other,))
         if n:
-            for s in waves[n - 1]:
-                outbox[s] = total(s)
+            sums = [total(s) for s in waves[n - 1]]
+            for s, value in zip(waves[n - 1], sums):
+                outbox[s] = value
             deliver(waves[n - 1])
     sums = [total(s) for s in waves[-1]]
     for s, value in zip(waves[-1], sums):
         outbox[s] = value
-    inbox[c, 0] = sums[-1]
     deliver(waves[-1])
+
+    match((0,), UP1, 7, both)
+    own = total(0)
+    outbox[0] = own
+    inbox[c, 0] = own
+
     sibling = pltpu.make_async_remote_copy(
         src_ref=outbox.at[0], dst_ref=inbox.at[c, 0], send_sem=ssend.at[0, 0], recv_sem=srecv.at[c, 0],
         device_id={"tok": other}, device_id_type=MESH,

time: 35.8 us -> 34.2 us (0.955)
  Pallas kernels: 34.4 us -> 32.8 us
    pallas_call x1, Pallas kernels: 34.4 us -> 32.8 us  [body(): pl.pallas_call(kernel, out_shape=jax.ShapeDtypeStruct((16, 128), jnp.floa...]
where the time goes in v4:
time: 34.2 us; the launch traced here: 34.1 us
  Pallas kernels  32.8 us (96%)
  local copies, waits for them, and re-layouts  1.3 us (4%)
    pallas_call x1, Pallas kernels, body(): pl.pallas_call(kernel, out_shape=jax.ShapeDtypeStruct((16, 128), jnp.floa...  32.8 us
    unnamed x1, local copies, waits for them, and re-layouts  1.3 us

profile of v4, /device:TPU:1, one launch (start us, length us, event | category | flops | bytes accessed | tf_op | source)
XLA Modules:
  0.0 34.1 jit_solution(7355640264099755177)
XLA Ops:
  0.0 32.8 %shard_map.46 = f32[16,128]{1,0:T(8,128)} custom-call(bf16[16,16,128]{2,1,0:T(8,128)(2,1)} %q_hbm.1, bf16[4,128,128]{2,1,0:T(8,128)(2,1)} %d_hbm.1, s32[4]{0:T(128)} %len_hbm.1, s32[2,256]{1,0:T(2,128)} %cand_hbm.1), custom_call_target="tpu_custom_call" | custom-call | tf_op jit(solution)/shard_map/pallas_call | solution.py:394
  32.8 1.3 %copy.6 = f32[16,128]{1,0:T(8,128)} copy(f32[16,128]{1,0:T(8,128)} %shard_map.46) | data formatting | bytes 16384

commit v5 on v4

--- a/solution.py
+++ b/solution.py
@@ -266,17 +266,16 @@
     for part in (1, 0):
         z_wait(DN3, part)
     share(DN3)
-    for s in far[:2]:
+    match(inner + corner, UP3, 2, (c,))
+    for s in far:
         q_wait(s, 0)
         q_wait(s, 1)
     z_wait(FAR, 0)
     z_wait(FAR, 1)
     share(FAR)
-    for s in far[2:]:
-        q_wait(s, 0)
-        q_wait(s, 1)
     match(far, OWN, 5, both)
-    match(range(1, 16), UP3, 3, (c,))
+    match(far, UP3, 3, (c,))
+    match(inner + corner, FAR, 1, (c,))
     share_wait(UP3)
     share_wait(DN3)
     share_wait(FAR)

time: 34.2 us -> 34.3 us (level)
  no operation moved by 1% of the time
where the time goes in v5:
time: 34.3 us; the launch traced here: 34.1 us
  Pallas kernels  32.8 us (96%)
  local copies, waits for them, and re-layouts  1.3 us (4%)
    pallas_call x1, Pallas kernels, body(): pl.pallas_call(kernel, out_shape=jax.ShapeDtypeStruct((16, 128), jnp.floa...  32.8 us
    unnamed x1, local copies, waits for them, and re-layouts  1.3 us

profile of v5, /device:TPU:1, one launch (start us, length us, event | category | flops | bytes accessed | tf_op | source)
XLA Modules:
  0.0 34.1 jit_solution(11987587889051028832)
XLA Ops:
  0.0 32.8 %shard_map.46 = f32[16,128]{1,0:T(8,128)} custom-call(bf16[16,16,128]{2,1,0:T(8,128)(2,1)} %q_hbm.1, bf16[4,128,128]{2,1,0:T(8,128)(2,1)} %d_hbm.1, s32[4]{0:T(128)} %len_hbm.1, s32[2,256]{1,0:T(2,128)} %cand_hbm.1), custom_call_target="tpu_custom_call" | custom-call | tf_op jit(solution)/shard_map/pallas_call | solution.py:393
  32.8 1.3 %copy.6 = f32[16,128]{1,0:T(8,128)} copy(f32[16,128]{1,0:T(8,128)} %shard_map.46) | data formatting | bytes 16384
